TPU v7x, 32 devices: a whole 2x2x4 slice. The times are simulated.
32 devices in a mesh: groups: 2 (over y), nodes: 16 (over z, x, core).
Axes of the slice: x: 2, y: 2, z: 4, core: 2. Of those that a mesh axis runs over, the one named last changes fastest.
Arguments:
- grid_feats: bfloat16 [32768, 1024], P(('groups', 'nodes')), parts along dimension 0, may hold values from -6 to 6
- mesh_feats: bfloat16 [4096, 1024], P(('groups', 'nodes')), parts along dimension 0, may hold values from -6 to 6
- mesh_cot: bfloat16 [4096, 1024], P(('groups', 'nodes')), parts along dimension 0, may hold values from -6 to 6
- w_src: bfloat16 [1024, 1024], replicated, may hold values from -0.1875 to 0.1875
- w_dst: bfloat16 [1024, 1024], replicated, may hold values from -0.1875 to 0.1875
- w_out: bfloat16 [1024, 1024], replicated, may hold values from -0.1875 to 0.1875
- edge_bias: float32 [1024], replicated, may hold values from -4 to 4
- tile_src: int32 [192], P(('groups', 'nodes')), parts along dimension 0, may hold values from 0 to 7
- tile_rows: int32 [192, 128], P(('groups', 'nodes')), parts along dimension 0, may hold values from 0 to 128, as said below
- tile_count: int32 [96], P(('groups', 'nodes')), parts along dimension 0, may hold values from 0 to 2, as said below
Outputs:
- mesh_out: bfloat16 [4096, 1024], P(('groups', 'nodes')), parts along dimension 0
- grid_grad: bfloat16 [32768, 1024], P(('groups', 'nodes')), parts along dimension 0
- mesh_grad: bfloat16 [4096, 1024], P(('groups', 'nodes')), parts along dimension 0
There are 2 independent parts, one for each index of `groups`. A program takes and returns all parts, laid end to end along the dimension named above; an argument that names none is the same for every part. Nothing has to cross between parts.
Inputs may be any that keep to these rules, and one draw needn't show every extreme that they name: `tile_count`: tile slots of a device and destination beyond its count carry no edges. `tile_rows`: the value 128 marks a grid point of a tile without an edge.
All inputs are finite; a program needn't handle non-finite values.
Results may differ from a plain program's by a relative error of at most 0.0051.
Values may be sent and summed in bfloat16 or wider, within the bound.
A program may use at most 64 MiB of HBM per device.

v0:
```python
import jax
import jax.numpy as jnp
from jax import lax
from jax.sharding import PartitionSpec as P


def passed_along(value, axis, steps):
    count = lax.axis_size(axis)
    pairs = [(source, (source + steps) % count) for source in range(count)]
    return lax.ppermute(value, axis, pairs)


def silu_slope(value):
    sig = jax.nn.sigmoid(value)
    return sig * (1.0 + value * (1.0 - sig))


def src_grad(pre_grad, w_src):
    return lax.dot_general(
        pre_grad, w_src, (((1,), (1,)), ((), ())), preferred_element_type=jnp.float32
    )


def edge_terms(flat_feats, h_proj, g_proj, onehot, edge_mask, w_src, w_out, edge_bias):
    h_pick = jnp.dot(
        onehot, h_proj, precision=lax.Precision.HIGHEST, preferred_element_type=jnp.float32
    )
    g_pick = jnp.dot(
        onehot, g_proj, precision=lax.Precision.HIGHEST, preferred_element_type=jnp.float32
    )
    pre_act = jnp.dot(flat_feats, w_src, preferred_element_type=jnp.float32) + edge_bias + h_pick
    hidden_act = jax.nn.silu(pre_act).astype(jnp.bfloat16)
    message = jnp.dot(hidden_act, w_out, preferred_element_type=jnp.float32) * edge_mask
    pre_grad = (g_pick * silu_slope(pre_act) * edge_mask).astype(jnp.bfloat16)
    return (message, pre_grad)


def row_sums(onehot, message, pre_grad):
    mesh_sum = lax.dot_general(
        onehot,
        message,
        (((0,), (0,)), ((), ())),
        precision=lax.Precision.HIGHEST,
        preferred_element_type=jnp.float32,
    )
    pre_sum = lax.dot_general(
        onehot.astype(jnp.bfloat16),
        pre_grad,
        (((0,), (0,)), ((), ())),
        preferred_element_type=jnp.float32,
    )
    return (mesh_sum, pre_sum)


def local(
    grid_feats,
    mesh_feats,
    mesh_cot,
    w_src,
    w_dst,
    w_out,
    edge_bias,
    tile_src,
    tile_rows,
    tile_count,
):
    block_len = tile_rows.shape[1]
    width = grid_feats.shape[1]
    grid_blocks = grid_feats.shape[0] // block_len
    offsets = tile_count.shape[0]
    capacity = tile_src.shape[0] // offsets
    tile_slots = offsets * capacity
    own_offset = offsets // 2
    x_blocks = grid_feats.reshape(grid_blocks, block_len, width)
    slot_off = jnp.repeat(jnp.arange(offsets, dtype=jnp.int32), capacity)
    slot_pos = jnp.tile(jnp.arange(capacity, dtype=jnp.int32), offsets)
    alive_mask = (slot_pos < tile_count[slot_off])[:, None] & (tile_rows < block_len)
    edge_row = jnp.where(alive_mask, tile_rows, block_len)
    tile_feats = x_blocks[tile_src]
    feat_list = []
    row_list = []
    for offset in range(offsets):
        part_feats = tile_feats[offset * capacity : (offset + 1) * capacity]
        part_rows = edge_row[offset * capacity : (offset + 1) * capacity]
        if offset == own_offset:
            feat_list.append(part_feats)
            row_list.append(part_rows)
        else:
            got_feats, got_rows = passed_along(
                (part_feats, part_rows), "nodes", offset - own_offset
            )
            feat_list.append(got_feats)
            row_list.append(got_rows)
    in_feats = jnp.concatenate(feat_list, axis=0).reshape(-1, width)
    in_rows = jnp.concatenate(row_list, axis=0).reshape(-1)
    h_proj = jnp.dot(mesh_feats, w_dst, preferred_element_type=jnp.float32)
    g_proj = lax.dot_general(
        mesh_cot, w_out, (((1,), (1,)), ((), ())), preferred_element_type=jnp.float32
    )
    edge_mask = (in_rows < block_len).astype(jnp.float32)[:, None]
    pick_rows = jnp.minimum(in_rows, block_len - 1)
    onehot = (pick_rows[:, None] == jnp.arange(block_len, dtype=jnp.int32)[None, :]).astype(
        jnp.float32
    )
    message, pre_grad = edge_terms(
        in_feats, h_proj, g_proj, onehot, edge_mask, w_src, w_out, edge_bias
    )
    mesh_sum, pre_sum = row_sums(onehot, message, pre_grad)
    grad_tiles = src_grad(pre_grad, w_src).reshape(tile_slots, block_len, width)
    home_list = []
    for offset in range(offsets):
        part_grad = grad_tiles[offset * capacity : (offset + 1) * capacity]
        if offset == own_offset:
            home_list.append(part_grad)
        else:
            home_list.append(passed_along(part_grad, "nodes", own_offset - offset))
    home_grad = jnp.concatenate(home_list, axis=0)
    block_grad = jnp.zeros((grid_blocks, block_len, width), jnp.float32).at[tile_src].add(home_grad)
    grid_grad = block_grad.astype(jnp.bfloat16).reshape(grid_blocks * block_len, width)
    mesh_out = (mesh_feats.astype(jnp.float32) + mesh_sum).astype(jnp.bfloat16)
    pre_round = pre_sum.astype(jnp.bfloat16)
    mesh_grad = (
        mesh_cot.astype(jnp.float32)
        + lax.dot_general(
            pre_round, w_dst, (((1,), (1,)), ((), ())), preferred_element_type=jnp.float32
        )
    ).astype(jnp.bfloat16)
    return (mesh_out, grid_grad, mesh_grad)


def solution(mesh):
    placed = (
        P(("groups", "nodes"), None),
        P(("groups", "nodes"), None),
        P(("groups", "nodes"), None),
        P(),
        P(),
        P(),
        P(),
        P(("groups", "nodes")),
        P(("groups", "nodes"), None),
        P(("groups", "nodes")),
    )
    return jax.shard_map(
        local,
        mesh=mesh,
        in_specs=placed,
        out_specs=(
            P(("groups", "nodes"), None),
            P(("groups", "nodes"), None),
            P(("groups", "nodes"), None),
        ),
        check_vma=False,
    )
```

profile of v0, /device:TPU:1, one launch (start us, length us, event | category | flops | bytes accessed | tf_op | source)
XLA Modules:
  0.0 77.6 jit_solution(15143926581746767665)
XLA Ops:
  0.6 0.0 copy-start
  0.7 0.1 reshape.76
  0.7 0.1 tile.10
  0.8 1.4 %gather_fusion = s32[6]{0:T(128)S(1)} fusion(s32[3]{0:T(128)} %param.19, s32[1024]{0:T(1024)S(1)} %pad_clamp_fusion.1), kind=kCustom, calls=%fused_computation | custom fusion | bytes 72 | tf_op jit(solution)/shard_map/gather | solution.py:77
  2.3 0.8 and_select_fusion
  3.0 0.1 collective-permute-start
  3.1 2.6 %collective-permute-start.1 = (s32[2,128]{1,0:T(2,128)S(1)}, s32[2,128]{1,0:T(2,128)S(1)}, u32[]{:S(2)}, u32[]{:S(2)}) collective-permute-start(s32[2,128]{1,0:T(2,128)S(1)} %get-tuple-element.10), channel_id=1, source_target_pairs={{0,1},{1,2},{2,3},{3,4},{4,5},{5,6},{6,7},{7,8},{8,9},{9,10},{10,1... | collective-permute-start | bytes 3080 | tf_op jit(solution)/shard_map/ppermute | solution.py:10
  5.7 0.7 compare_select_fusion
  6.4 0.0 copy-done
  6.4 0.0 copy-start.4
  6.4 1.8 %gather_fusion.1 = bf16[6,128,1024]{2,1,0:T(8,128)(2,1)} fusion(bf16[8,128,1024]{2,1,0:T(8,128)(2,1)S(1)} %bitcast.25, s32[1024]{0:T(1024)S(1)} %pad_clamp_fusion), kind=kCustom, calls=%fused_computation.1 | custom fusion | bytes 3145752 | tf_op jit(solution)/shard_map/gather | solution.py:79
  8.2 0.0 copy-start.2
  8.2 1.6 %fusion.20 = (bf16[2,128,1024]{2,1,0:T(8,128)(2,1)S(1)}, bf16[2,128,1024]{2,1,0:T(8,128)(2,1)S(1)}, bf16[2,128,1024]{2,1,0:T(8,128)(2,1)S(1)}) fusion(bf16[6,128,1024]{2,1,0:T(8,128)(2,1)} %gather_fusion.1), kind=kLoop, calls=%fused_computation.36 | loop fusion | bytes 3145728 | tf_op jit(solution)/shard_map/slice | solution.py:83
  9.8 2.9 %collective-permute-start.2 = (bf16[2,128,1024]{2,1,0:T(8,128)(2,1)S(1)}, bf16[2,128,1024]{2,1,0:T(8,128)(2,1)S(1)}, u32[]{:S(2)}, u32[]{:S(2)}) collective-permute-start(bf16[2,128,1024]{2,1,0:T(8,128)(2,1)S(1)} %get-tuple-element.6), channel_id=1, source_target_pairs={{0,15},{1,0},{2,1},{3,2},{4,3},{5,4},{6,5},{7,6},{8,7},{9,8},{10,9... | collective-permute-start | bytes 1572872 | tf_op jit(solution)/shard_map/ppermute | solution.py:10
  12.7 0.0 collective-permute-start.3
  12.7 0.0 copy-done.4
  12.7 0.0 copy-done.1
  12.7 0.4 fusion.22
  13.2 0.0 copy-done.2
  13.2 0.0 copy-done.5
  13.2 0.8 %fusion.23 = f32[128,1024]{1,0:T(8,128)S(1)} fusion(bf16[128,1024]{1,0:T(8,128)(2,1)S(1)} %copy-done.5, bf16[1024,1024]{1,0:T(8,128)(2,1)S(1)} %copy-done.2), kind=kOutput, calls=%fused_computation.39 | convolution fusion | flops 268435456 | bytes 2883584 | tf_op jit(solution)/shard_map/dot_general | solution.py:97
  14.1 0.0 collective-permute-done
  14.1 0.0 collective-permute-done.1
  14.1 0.0 copy-start.6
  14.1 0.0 copy-start.7
  14.1 1.5 %fusion.11 = f32[768,1024]{1,0:T(8,128)S(1)} fusion(f32[128,1024]{1,0:T(8,128)S(1)} %fusion.22, s32[768]{0:T(1024)S(1)} %minimum_bitcast_fusion), kind=kOutput, calls=%fused_computation.20 | convolution fusion | flops 1208057856 | bytes 3673088 | tf_op jit(solution)/shard_map/dot_general | solution.py:25
  15.6 2.9 %collective-permute-done.2 = bf16[2,128,1024]{2,1,0:T(8,128)(2,1)S(1)} collective-permute-done((bf16[2,128,1024]{2,1,0:T(8,128)(2,1)S(1)}, bf16[2,128,1024]{2,1,0:T(8,128)(2,1)S(1)}, u32[]{:S(2)}, u32[]{:S(2)}) %collective-permute-start.2) | collective-permute-done | bytes 524320 | tf_op jit(solution)/shard_map/ppermute | solution.py:10
  18.5 6.0 %collective-permute-done.3 = bf16[2,128,1024]{2,1,0:T(8,128)(2,1)S(1)} collective-permute-done((bf16[2,128,1024]{2,1,0:T(8,128)(2,1)S(1)}, bf16[2,128,1024]{2,1,0:T(8,128)(2,1)S(1)}, u32[]{:S(2)}, u32[]{:S(2)}) %collective-permute-start.3) | collective-permute-done | bytes 524320 | tf_op jit(solution)/shard_map/ppermute | solution.py:10
  24.5 0.2 pad_maximum_fusion.1
  24.6 0.0 copy-done.6
  24.7 0.0 copy-done.7
  24.7 1.8 %add_add_fusion = f32[768,1024]{1,0:T(8,128)S(1)} fusion(f32[768,1024]{1,0:T(8,128)S(1)} %fusion.11, bf16[768,1024]{1,0:T(8,128)(2,1)S(1)} %bitcast.28, bf16[1024,1024]{1,0:T(8,128)(2,1)S(1)} %copy-done.6, f32[1024]{0:T(1024)S(1)} %copy-done.7), kind=kOutput, calls=%fused_computation.9 | convolution fusion | flops 1612185600 | bytes 9965568 | tf_op jit(solution)/shard_map/dot_general | solution.py:31
  26.5 2.7 %multiply_convert_fusion = bf16[768,1024]{1,0:T(8,128)(2,1)S(1)} fusion(f32[768,1024]{1,0:T(8,128)S(1)} %add_add_fusion, f32[128,1024]{1,0:T(8,128)S(1)} %fusion.23, f32[768]{0:T(1024)S(1)} %convert_bitcast_fusion, s32[768]{0:T(1024)S(1)} %minimum_bitcast_fusion), kind=kOutput, calls=%fused_computation.4 | convolution fusion | flops 1215922176 | bytes 5249024 | tf_op jit(solution)/shard_map/dot_general | solution.py:28
  29.3 0.0 copy-start.3
  29.3 1.8 %fusion.24 = f32[768,1024]{1,0:T(8,128)S(1)} fusion(bf16[768,1024]{1,0:T(8,128)(2,1)S(1)} %multiply_convert_fusion, bf16[1024,1024]{1,0:T(8,128)(2,1)S(1)} %copy-done.6), kind=kOutput, calls=%fused_computation.40 | convolution fusion | flops 1610612736 | bytes 6815744 | tf_op jit(solution)/shard_map/dot_general | solution.py:19
  31.1 0.0 copy-done.3
  31.1 1.5 %fusion.19 = (f32[256,1024]{1,0:T(8,128)}, f32[256,1024]{1,0:T(8,128)}, f32[256,1024]{1,0:T(8,128)S(1)}) fusion(f32[768,1024]{1,0:T(8,128)S(1)} %fusion.24), kind=kLoop, calls=%fused_computation.35 | loop fusion | bytes 6291456 | tf_op jit(solution)/shard_map/slice | solution.py:112
  32.7 4.0 %collective-permute-start.5 = (f32[2,128,1024]{2,1,0:T(8,128)}, f32[2,128,1024]{2,1,0:T(8,128)}, u32[]{:S(2)}, u32[]{:S(2)}) collective-permute-start(f32[2,128,1024]{2,1,0:T(8,128)} %bitcast.7), channel_id=1, source_target_pairs={{0,15},{1,0},{2,1},{3,2},{4,3},{5,4},{6,5},{7,6},{8,7},{9,8},{10,9... | collective-permute-start | bytes 3145736 | tf_op jit(solution)/shard_map/ppermute | solution.py:10
  36.7 0.0 collective-permute-start.4
  36.7 1.8 %fusion.3 = f32[768,1024]{1,0:T(8,128)S(1)} fusion(bf16[1024,1024]{1,0:T(8,128)(2,1)S(1)} %copy-done.2, f32[768,1024]{1,0:T(8,128)S(1)} %add_add_fusion), kind=kOutput, calls=%fused_computation.12 | convolution fusion | flops 1614544896 | bytes 8388608 | tf_op jit(solution)/shard_map/dot_general | solution.py:33
  38.5 2.2 %fusion.7 = bf16[128,1024]{1,0:T(8,128)(2,1)} fusion(f32[768,1024]{1,0:T(8,128)S(1)} %fusion.3, f32[768]{0:T(1024)S(1)} %convert_bitcast_fusion, bf16[128,1024]{1,0:T(8,128)(2,1)S(1)} %copy-done.4, s32[768]{0:T(1024)S(1)} %minimum_bitcast_fusion), kind=kOutput, calls=%fused_computation.15 | convolution fusion | flops 1209237504 | bytes 3676160 | tf_op jit(solution)/shard_map/dot_general | solution.py:39
  40.7 4.0 %fusion.10 = bf16[128,1024]{1,0:T(8,128)(2,1)} fusion(bf16[1024,1024]{1,0:T(8,128)(2,1)} %param.14, bf16[768,1024]{1,0:T(8,128)(2,1)} %copy-done.3, bf16[128,1024]{1,0:T(8,128)(2,1)} %param.12, s32[768]{0:T(1024)S(1)} %minimum_bitcast_fusion), kind=kOutput, calls=%fused_computation.17 | convolution fusion | flops 470581248 | bytes 4197376 | tf_op jit(solution)/shard_map/dot_general | solution.py:124
  44.8 14.4 %collective-permute-done.5 = f32[2,128,1024]{2,1,0:T(8,128)} collective-permute-done((f32[2,128,1024]{2,1,0:T(8,128)}, f32[2,128,1024]{2,1,0:T(8,128)}, u32[]{:S(2)}, u32[]{:S(2)}) %collective-permute-start.5) | collective-permute-done | bytes 1048608 | tf_op jit(solution)/shard_map/ppermute | solution.py:10
  59.2 0.0 collective-permute-done.4
  59.2 3.6 %pad_maximum_fusion = f32[6,128,1024]{2,1,0:T(8,128)} fusion(f32[2,128,1024]{2,1,0:T(8,128)} %collective-permute-done.5, f32[2,128,1024]{2,1,0:T(8,128)S(1)} %bitcast.26, f32[2,128,1024]{2,1,0:T(8,128)} %collective-permute-done.4), kind=kLoop, calls=%fused_computation.3 | loop fusion | flops 1572864 | bytes 6291456 | tf_op jit(solution)/shard_map/concatenate | solution.py:117
  62.8 2.5 %broadcast_in_dim.10 = f32[8,128,1024]{2,1,0:T(8,128)} broadcast(f32[]{:T(128)} %constant.4.clone.1), dimensions={} | broadcast | bytes 4194308 | tf_op jit(solution)/shard_map/broadcast_in_dim | solution.py:118
  65.2 8.5 %scatter_fusion = f32[8,128,1024]{2,1,0:T(8,128)} fusion(f32[8,128,1024]{2,1,0:T(8,128)} %broadcast_in_dim.10, s32[6]{0:T(128)S(1)} %compare_select_fusion, f32[6,128,1024]{2,1,0:T(8,128)} %pad_maximum_fusion), kind=kCustom, calls=%fused_computation.2 | custom fusion | flops 786432 | bytes 9437208 | tf_op jit(solution)/shard_map/scatter-add | solution.py:118
  73.7 3.8 %convert_element_type.46 = bf16[8,128,1024]{2,1,0:T(8,128)(2,1)} convert(f32[8,128,1024]{2,1,0:T(8,128)} %scatter_fusion) | non-fusion elementwise | flops 1048576 | bytes 6291456 | tf_op jit(solution)/shard_map/convert_element_type | solution.py:119
  (11 shorter events, 0.1 us)
Async XLA Ops:
  0.6 5.7 %copy-start = (bf16[1024,1024]{1,0:T(8,128)(2,1)S(1)}, bf16[1024,1024]{1,0:T(8,128)(2,1)}, u32[]{:S(2)}) copy-start(bf16[1024,1024]{1,0:T(8,128)(2,1)} %param.10) | copy-start | bytes 6291460
  3.0 11.0 %collective-permute-start = (s32[2,128]{1,0:T(2,128)S(1)}, s32[2,128]{1,0:T(2,128)S(1)}, u32[]{:S(2)}, u32[]{:S(2)}) collective-permute-start(s32[2,128]{1,0:T(2,128)S(1)} %get-tuple-element.9), channel_id=1, source_target_pairs={{0,15},{1,0},{2,1},{3,2},{4,3},{5,4},{6,5},{7,6},{8,7},{9,8},{10,9... | collective-permute-start | bytes 3080 | tf_op jit(solution)/shard_map/ppermute | solution.py:10
  3.1 11.0 %collective-permute-start.1 = (s32[2,128]{1,0:T(2,128)S(1)}, s32[2,128]{1,0:T(2,128)S(1)}, u32[]{:S(2)}, u32[]{:S(2)}) collective-permute-start(s32[2,128]{1,0:T(2,128)S(1)} %get-tuple-element.10), channel_id=1, source_target_pairs={{0,1},{1,2},{2,3},{3,4},{4,5},{5,6},{6,7},{7,8},{8,9},{9,10},{10,1... | collective-permute-start | bytes 3080 | tf_op jit(solution)/shard_map/ppermute | solution.py:10
  6.4 6.4 %copy-start.4 = (bf16[128,1024]{1,0:T(8,128)(2,1)S(1)}, bf16[128,1024]{1,0:T(8,128)(2,1)}, u32[]{:S(2)}) copy-start(bf16[128,1024]{1,0:T(8,128)(2,1)} %param.11) | copy-start | bytes 786436
  8.2 4.5 %copy-start.1 = (bf16[1024,1024]{1,0:T(8,128)(2,1)S(1)}, bf16[1024,1024]{1,0:T(8,128)(2,1)}, u32[]{:S(2)}) copy-start(bf16[1024,1024]{1,0:T(8,128)(2,1)} %param.14) | copy-start | bytes 6291460
  8.2 5.0 %copy-start.2 = (bf16[1024,1024]{1,0:T(8,128)(2,1)S(1)}, bf16[1024,1024]{1,0:T(8,128)(2,1)}, u32[]{:S(2)}) copy-start(bf16[1024,1024]{1,0:T(8,128)(2,1)} %param.15) | copy-start | bytes 6291460
  8.2 5.0 %copy-start.5 = (bf16[128,1024]{1,0:T(8,128)(2,1)S(1)}, bf16[128,1024]{1,0:T(8,128)(2,1)}, u32[]{:S(2)}) copy-start(bf16[128,1024]{1,0:T(8,128)(2,1)} %param.12) | copy-start | bytes 786436
  9.8 8.7 %collective-permute-start.2 = (bf16[2,128,1024]{2,1,0:T(8,128)(2,1)S(1)}, bf16[2,128,1024]{2,1,0:T(8,128)(2,1)S(1)}, u32[]{:S(2)}, u32[]{:S(2)}) collective-permute-start(bf16[2,128,1024]{2,1,0:T(8,128)(2,1)S(1)} %get-tuple-element.6), channel_id=1, source_target_pairs={{0,15},{1,0},{2,1},{3,2},{4,3},{5,4},{6,5},{7,6},{8,7},{9,8},{10,9... | collective-permute-start | bytes 1572872 | tf_op jit(solution)/shard_map/ppermute | solution.py:10
  12.7 11.7 %collective-permute-start.3 = (bf16[2,128,1024]{2,1,0:T(8,128)(2,1)S(1)}, bf16[2,128,1024]{2,1,0:T(8,128)(2,1)S(1)}, u32[]{:S(2)}, u32[]{:S(2)}) collective-permute-start(bf16[2,128,1024]{2,1,0:T(8,128)(2,1)S(1)} %get-tuple-element.8), channel_id=1, source_target_pairs={{0,1},{1,2},{2,3},{3,4},{4,5},{5,6},{6,7},{7,8},{8,9},{9,10},{10,1... | collective-permute-start | bytes 1572872 | tf_op jit(solution)/shard_map/ppermute | solution.py:10
  14.1 10.5 %copy-start.6 = (bf16[1024,1024]{1,0:T(8,128)(2,1)S(1)}, bf16[1024,1024]{1,0:T(8,128)(2,1)}, u32[]{:S(2)}) copy-start(bf16[1024,1024]{1,0:T(8,128)(2,1)} %param.13) | copy-start | bytes 6291460
  14.1 10.5 %copy-start.7 = (f32[1024]{0:T(1024)S(1)}, f32[1024]{0:T(1024)}, u32[]{:S(2)}) copy-start(f32[1024]{0:T(1024)} %param.16) | copy-start | bytes 12292
  29.3 1.9 %copy-start.3 = (bf16[768,1024]{1,0:T(8,128)(2,1)}, bf16[768,1024]{1,0:T(8,128)(2,1)S(1)}, u32[]{:S(2)}) copy-start(bf16[768,1024]{1,0:T(8,128)(2,1)S(1)} %multiply_convert_fusion) | copy-start | bytes 4718596
  32.7 26.5 %collective-permute-start.5 = (f32[2,128,1024]{2,1,0:T(8,128)}, f32[2,128,1024]{2,1,0:T(8,128)}, u32[]{:S(2)}, u32[]{:S(2)}) collective-permute-start(f32[2,128,1024]{2,1,0:T(8,128)} %bitcast.7), channel_id=1, source_target_pairs={{0,15},{1,0},{2,1},{3,2},{4,3},{5,4},{6,5},{7,6},{8,7},{9,8},{10,9... | collective-permute-start | bytes 3145736 | tf_op jit(solution)/shard_map/ppermute | solution.py:10
  36.7 22.5 %collective-permute-start.4 = (f32[2,128,1024]{2,1,0:T(8,128)}, f32[2,128,1024]{2,1,0:T(8,128)}, u32[]{:S(2)}, u32[]{:S(2)}) collective-permute-start(f32[2,128,1024]{2,1,0:T(8,128)} %bitcast.5), channel_id=1, source_target_pairs={{0,1},{1,2},{2,3},{3,4},{4,5},{5,6},{6,7},{7,8},{8,9},{9,10},{10,1... | collective-permute-start | bytes 3145736 | tf_op jit(solution)/shard_map/ppermute | solution.py:10
where the time goes:
time: 77.9 us; the launch traced here: 77.6 us
  waiting for transfers between devices  23.3 us (30%)
  other arithmetic  17.6 us (23%)
  matrix products  17.3 us (22%)
  starting transfers between devices  9.53 us (12%)
  local copies, waits for them, and re-layouts  9.12 us (12%)
  between operations  0.82 us (1%)
    ppermute x6, waiting for transfers between devices, passed_along(): return lax.ppermute(value, axis, pairs)  23.3 us
    ppermute x6, starting transfers between devices, passed_along(): return lax.ppermute(value, axis, pairs)  9.53 us
    scatter-add x1, other arithmetic, local(): jnp.zeros((grid_blocks, block_len, width), jnp.float32).at[tile_src]  8.51 us
    dot_general x1, matrix products, local(): lax.dot_general(pre_round, w_dst, (((1,), (1,)), ((), ())), preferred_ele...  4.05 us
    convert_element_type x1, other arithmetic, local(): block_grad.astype(jnp.bfloat16).reshape(grid_blocks * block_len, width)  3.84 us
    concatenate x1, other arithmetic, local(): home_grad = jnp.concatenate(home_list, axis=0)  3.58 us
    dot_general x1, matrix products, edge_terms(): jnp.dot(onehot, g_proj, precision=lax.Precision.HIGHEST, preferred_elemen...  2.73 us
    broadcast_in_dim x1, local copies, waits for them, and re-layouts, local(): jnp.zeros((grid_blocks, block_len, width), jnp.float32).at[tile_src]  2.47 us
  transfers between devices with their start and end apart: 6, of which 3 were waited for; matrix products, arithmetic and copies ran while one was open for 19% of the time, Pallas kernels for 0%

commit v1 on v0

v1 whole, which is shorter than its diff:
```python
import functools

import jax
import jax.numpy as jnp
from jax import lax
from jax.experimental import pallas as pl
from jax.experimental.pallas import tpu as pltpu
from jax.sharding import PartitionSpec as P

NODES = "nodes"
COLS = 256
F32 = jnp.float32
BF16 = jnp.bfloat16


def nt_dot(a, b):
    return lax.dot_general(a, b, (((1,), (1,)), ((), ())), preferred_element_type=F32)


def nn_dot(a, b):
    return jnp.dot(a, b, preferred_element_type=F32)


def high_low(value):
    high = value.astype(BF16)
    low = (value - high.astype(F32)).astype(BF16)
    return jnp.concatenate([high, low], axis=0)


def kernel(
    n,
    tile_src,
    tile_count,
    rows_ref,
    bias_ref,
    x_hbm,
    feats_hbm,
    cot_hbm,
    wsrc_hbm,
    wdst_hbm,
    wout_hbm,
    mesh_out,
    grid_grad,
    mesh_grad,
    x_v,
    wsrc,
    wdst,
    wout,
    feats,
    cot,
    xt,
    pre,
    pg,
    spread,
    pick,
    s_own,
    p_own,
    s_send,
    p_send,
    feats_in,
    cot_in,
    s_in,
    p_in,
    gt,
    gg,
    mo,
    mg,
    load_sem,
    store_sem,
    send_sem,
    recv_sem,
):
    blk = rows_ref.shape[1]
    slots = rows_ref.shape[0]
    offs = tile_count.shape[0]
    cap = slots // offs
    own = offs // 2
    width = x_v.shape[1]
    hidden_width = wsrc.shape[1]
    grid_blocks = x_v.shape[0] // blk
    per = cap * blk

    me = lax.axis_index(NODES)
    right = lax.rem(me + 1, n)
    left = lax.rem(me + n - 1, n)

    def load(i, src, dst):
        copy = pltpu.make_async_copy(src, dst, load_sem.at[i])
        copy.start()
        return copy

    load_x = load(0, x_hbm, x_v)
    load_wsrc = load(1, wsrc_hbm, wsrc)
    load_feats = load(2, feats_hbm, feats)
    load_wdst = load(3, wdst_hbm, wdst)
    load_cot = load(4, cot_hbm, cot)
    load_wout = load(5, wout_hbm, wout)

    barrier = pltpu.get_barrier_semaphore()
    for neighbour in (left, right):
        pl.semaphore_signal(
            barrier, inc=1, device_id={NODES: neighbour}, device_id_type=pl.DeviceIdType.MESH
        )
    pl.semaphore_wait(barrier, 2)

    def send(kind, way, src, landing):
        return pltpu.make_async_remote_copy(
            src_ref=src,
            dst_ref=landing.at[way],
            send_sem=send_sem.at[kind, way],
            recv_sem=recv_sem.at[kind, way],
            device_id={NODES: right if way == 0 else left},
            device_id_type=pl.DeviceIdType.MESH,
        )

    feat_sends = [send(0, way, feats_hbm, feats_in) for way in range(2)]
    cot_sends = [send(1, way, cot_hbm, cot_in) for way in range(2)]
    s_sends = [send(2, way, s_send.at[way], s_in) for way in range(2)]
    p_sends = [send(3, way, p_send.at[way], p_in) for way in range(2)]
    for copy in feat_sends:
        copy.start()

    row_id = lax.broadcasted_iota(jnp.int32, (blk, blk), 0)
    for t in range(slots):
        o, c = t // cap, t % cap
        count = jnp.full((1, blk), tile_count[o], jnp.int32)
        rows = jnp.where(count > c, rows_ref[pl.ds(t, 1), :], blk)
        hit = jnp.where(row_id == rows, 1.0, 0.0).astype(F32)
        spread[o, :, c * blk : (c + 1) * blk] = hit.astype(BF16)
        turned = hit.T.astype(BF16)
        pick[t * blk : (t + 1) * blk, :blk] = turned
        pick[t * blk : (t + 1) * blk, blk:] = turned

    def chunk(i):
        return pl.ds(pl.multiple_of(i * COLS, COLS), COLS)

    def share(t, b):
        source = jnp.full((1, COLS), tile_src[t], jnp.int32)
        return jnp.where(source == b, 1.0, 0.0).astype(F32)

    load_x.wait()

    @pl.loop(0, width // COLS)
    def _(i):
        at = chunk(i)
        for t in range(slots):
            tile = share(t, 0).astype(BF16) * x_v[:blk, at]
            for b in range(1, grid_blocks):
                tile += share(t, b).astype(BF16) * x_v[b * blk : (b + 1) * blk, at]
            xt[t * blk : (t + 1) * blk, at] = tile

    load_wsrc.wait()

    @pl.loop(0, hidden_width // COLS)
    def _(i):
        at = chunk(i)
        pre[:, at] = nn_dot(xt[...], wsrc[:, at]) + bias_ref[:, at]

    def hidden_part(o, feats_ref, s_ref):
        lines = slice(o * per, (o + 1) * per)

        @pl.loop(0, hidden_width // COLS)
        def _(i):
            at = chunk(i)
            h = nn_dot(feats_ref[...], wdst[:, at])
            act = pre[lines, at] + nn_dot(pick[lines, :], high_low(h))
            sig = 0.5 * jnp.tanh(0.5 * act) + 0.5
            hidden = act * sig
            pre[lines, at] = sig + hidden * (1.0 - sig)
            s_ref[:, at] = nn_dot(spread[o], hidden.astype(BF16)).astype(s_ref.dtype)

    def grad_part(o, cot_ref, p_ref):
        lines = slice(o * per, (o + 1) * per)

        @pl.loop(0, hidden_width // COLS)
        def _(i):
            at = chunk(i)
            g = nt_dot(cot_ref[...], wout[at, :])
            grad = (nn_dot(pick[lines, :], high_low(g)) * pre[lines, at]).astype(BF16)
            pg[lines, at] = grad
            p_ref[:, at] = nn_dot(spread[o], grad).astype(p_ref.dtype)

    load_feats.wait()
    load_wdst.wait()
    hidden_part(own, feats, s_own)

    for way in range(2):
        feat_sends[way].wait_send()
        cot_sends[way].start()

    feat_sends[0].wait_recv()
    hidden_part(own - 1, feats_in.at[0], s_send.at[1])
    feat_sends[1].wait_recv()
    hidden_part(own + 1, feats_in.at[1], s_send.at[0])

    load_cot.wait()
    load_wout.wait()
    grad_part(own, cot, p_own)

    for way in range(2):
        cot_sends[way].wait_send()
        s_sends[way].start()

    cot_sends[0].wait_recv()
    grad_part(own - 1, cot_in.at[0], p_send.at[1])
    cot_sends[1].wait_recv()
    grad_part(own + 1, cot_in.at[1], p_send.at[0])

    for way in range(2):
        p_sends[way].start()

    @pl.loop(0, width // COLS)
    def _(i):
        at = chunk(i)
        gt[...] = nt_dot(pg[...], wsrc[at, :])
        for b in range(grid_blocks):
            total = share(0, b) * gt[:blk, :]
            for t in range(1, slots):
                total += share(t, b) * gt[t * blk : (t + 1) * blk, :]
            gg[b * blk : (b + 1) * blk, at] = total.astype(BF16)

    store_grid = pltpu.make_async_copy(gg, grid_grad, store_sem.at[0])
    store_grid.start()

    for way in range(2):
        s_sends[way].wait_recv()
    s_all = high_low(s_own[...] + s_in[0].astype(F32) + s_in[1].astype(F32))
    xt[: 2 * blk, :] = s_all

    @pl.loop(0, width // COLS)
    def _(i):
        at = chunk(i)
        both = nn_dot(xt[: 2 * blk, :], wout[:, at])
        mo[:, at] = (feats[:, at].astype(F32) + both[:blk] + both[blk:]).astype(BF16)

    store_mesh = pltpu.make_async_copy(mo, mesh_out, store_sem.at[1])
    store_mesh.start()

    for way in range(2):
        p_sends[way].wait_recv()
    xt[:blk, :] = (p_own[...] + p_in[0].astype(F32) + p_in[1].astype(F32)).astype(BF16)

    @pl.loop(0, width // COLS)
    def _(i):
        at = chunk(i)
        mg[:, at] = (cot[:, at].astype(F32) + nt_dot(xt[:blk, :], wdst[at, :])).astype(BF16)

    store_cot = pltpu.make_async_copy(mg, mesh_grad, store_sem.at[2])
    store_cot.start()
    for way in range(2):
        s_sends[way].wait_send()
        p_sends[way].wait_send()
    store_grid.wait()
    store_mesh.wait()
    store_cot.wait()


def local(
    grid_feats,
    mesh_feats,
    mesh_cot,
    w_src,
    w_dst,
    w_out,
    edge_bias,
    tile_src,
    tile_rows,
    tile_count,
):
    n = lax.axis_size(NODES)
    slots, blk = tile_rows.shape
    width = grid_feats.shape[1]
    hid = w_src.shape[1]
    offs = tile_count.shape[0]
    cap = slots // offs
    anywhere = pl.BlockSpec(memory_space=pl.ANY)
    outside = pl.BlockSpec(memory_space=pltpu.HBM)
    scalar = pl.BlockSpec(memory_space=pltpu.SMEM)
    vector = pl.BlockSpec(memory_space=pltpu.VMEM)
    flops = 2 * width * hid * (2 * slots * blk + 8 * blk)
    return pl.pallas_call(
        functools.partial(kernel, n),
        out_shape=(
            jax.ShapeDtypeStruct(mesh_feats.shape, BF16),
            jax.ShapeDtypeStruct(grid_feats.shape, BF16),
            jax.ShapeDtypeStruct(mesh_cot.shape, BF16),
        ),
        in_specs=[scalar, scalar, vector, vector] + [outside] * 6,
        out_specs=(anywhere, anywhere, anywhere),
        scratch_shapes=[
            pltpu.VMEM(grid_feats.shape, BF16),
            pltpu.VMEM(w_src.shape, BF16),
            pltpu.VMEM(w_dst.shape, BF16),
            pltpu.VMEM(w_out.shape, BF16),
            pltpu.VMEM((blk, width), BF16),
            pltpu.VMEM((blk, width), BF16),
            pltpu.VMEM((slots * blk, width), BF16),
            pltpu.VMEM((slots * blk, hid), F32),
            pltpu.VMEM((slots * blk, hid), BF16),
            pltpu.VMEM((offs, blk, cap * blk), BF16),
            pltpu.VMEM((slots * blk, 2 * blk), BF16),
            pltpu.VMEM((blk, hid), F32),
            pltpu.VMEM((blk, hid), F32),
            pltpu.VMEM((2, blk, hid), BF16),
            pltpu.VMEM((2, blk, hid), BF16),
            pltpu.VMEM((2, blk, width), BF16),
            pltpu.VMEM((2, blk, width), BF16),
            pltpu.VMEM((2, blk, hid), BF16),
            pltpu.VMEM((2, blk, hid), BF16),
            pltpu.VMEM((slots * blk, COLS), F32),
            pltpu.VMEM(grid_feats.shape, BF16),
            pltpu.VMEM((blk, width), BF16),
            pltpu.VMEM((blk, width), BF16),
            pltpu.SemaphoreType.DMA((6,)),
            pltpu.SemaphoreType.DMA((3,)),
            pltpu.SemaphoreType.DMA((4, 2)),
            pltpu.SemaphoreType.DMA((4, 2)),
        ],
        compiler_params=pltpu.CompilerParams(
            collective_id=0, has_side_effects=True, vmem_limit_bytes=44 * 1024 * 1024
        ),
        cost_estimate=pl.CostEstimate(
            flops=flops, bytes_accessed=12 * 1024 * 1024, transcendentals=slots * blk * hid
        ),
    )(
        tile_src,
        tile_count,
        tile_rows,
        edge_bias.reshape(1, hid),
        grid_feats,
        mesh_feats,
        mesh_cot,
        w_src,
        w_dst,
        w_out,
    )


def solution(mesh):
    both = P(("groups", NODES))
    wide = P(("groups", NODES), None)
    return jax.shard_map(
        local,
        mesh=mesh,
        in_specs=(wide, wide, wide, P(), P(), P(), P(), both, wide, both),
        out_specs=(wide, wide, wide),
        check_vma=False,
    )
```

time: 77.9 us -> 47.7 us (0.61)
  Pallas kernels: 0 us -> 34.6 us
  waiting for transfers between devices: 23.3 us -> 0 us
  other arithmetic: 17.6 us -> 0 us
  matrix products: 17.3 us -> 0 us
  starting transfers between devices: 9.53 us -> 0 us
  local copies, waits for them, and re-layouts: 9.12 us -> 12.1 us
    pallas_call x0 -> x1, Pallas kernels: none -> 34.6 us  [local(): pl.pallas_call(functools.partial(kernel, n), out_shape=(jax.ShapeDtypeStr...]
    ppermute x6 -> x0, waiting for transfers between devices: 23.3 us -> none  [passed_along(): return lax.ppermute(value, axis, pairs)]
    dot_general x9 -> x0, matrix products: 17.3 us -> none  [the longest x1 4.05 us: local(): lax.dot_general(pre_round, w_dst, (((1,), (1,)), ((), ())), preferred_ele...]
    unnamed x16 -> x21, local copies, waits for them, and re-layouts: 0.05 us -> 12.1 us
    ppermute x6 -> x0, starting transfers between devices: 9.53 us -> none  [passed_along(): return lax.ppermute(value, axis, pairs)]
    scatter-add x1 -> x0, other arithmetic: 8.51 us -> none  [local(): jnp.zeros((grid_blocks, block_len, width), jnp.float32).at[tile_src]]
    convert_element_type x2 -> x0, other arithmetic: 3.85 us -> none  [the longest x1 3.84 us: local(): block_grad.astype(jnp.bfloat16).reshape(grid_blocks * block_len, width)]
    concatenate x2 -> x0, other arithmetic: 3.75 us -> none  [the longest x1 3.58 us: local(): home_grad = jnp.concatenate(home_list, axis=0)]
  transfers between devices with their start and end apart: 6 -> 0, of which waited for: 3 -> 0; matrix products, arithmetic and copies ran while one was open for 19% -> 0% of each run, Pallas kernels for 0% -> 0%
where the time goes in v1:
time: 47.7 us; the launch traced here: 47.3 us
  Pallas kernels  34.6 us (73%)
  local copies, waits for them, and re-layouts  12.1 us (25%)
  between operations  0.66 us (1%)
    pallas_call x1, Pallas kernels, local(): pl.pallas_call(functools.partial(kernel, n), out_shape=(jax.ShapeDtypeStr...  34.6 us
    unnamed x21, local copies, waits for them, and re-layouts  12.1 us

profile of v1, /device:TPU:1, one launch (start us, length us, event | category | flops | bytes accessed | tf_op | source)
XLA Modules:
  0.0 47.3 jit_solution(14914203758629033293)
XLA Ops:
  0.6 0.0 copy-start
  0.6 1.6 %copy-done = bf16[1024,1024]{1,0:T(8,128)(2,1)S(1)} copy-done((bf16[1024,1024]{1,0:T(8,128)(2,1)S(1)}, bf16[1024,1024]{1,0:T(8,128)(2,1)}, u32[]{:S(2)}) %copy-start) | copy-done | bytes 2097176
  2.2 0.0 copy-start.1
  2.2 1.6 %copy-done.1 = bf16[1024,1024]{1,0:T(8,128)(2,1)S(1)} copy-done((bf16[1024,1024]{1,0:T(8,128)(2,1)S(1)}, bf16[1024,1024]{1,0:T(8,128)(2,1)}, u32[]{:S(2)}) %copy-start.1) | copy-done | bytes 2097176
  3.8 0.0 copy-start.2
  3.8 1.6 %copy-done.2 = bf16[1024,1024]{1,0:T(8,128)(2,1)S(1)} copy-done((bf16[1024,1024]{1,0:T(8,128)(2,1)S(1)}, bf16[1024,1024]{1,0:T(8,128)(2,1)}, u32[]{:S(2)}) %copy-start.2) | copy-done | bytes 2097176
  5.4 0.0 copy-start.3
  5.4 0.9 %copy-done.3 = bf16[128,1024]{1,0:T(8,128)(2,1)S(1)} copy-done((bf16[128,1024]{1,0:T(8,128)(2,1)S(1)}, bf16[128,1024]{1,0:T(8,128)(2,1)}, u32[]{:S(2)}) %copy-start.3) | copy-done | bytes 262168
  6.4 0.0 copy-start.4
  6.4 0.9 %copy-done.4 = bf16[128,1024]{1,0:T(8,128)(2,1)S(1)} copy-done((bf16[128,1024]{1,0:T(8,128)(2,1)S(1)}, bf16[128,1024]{1,0:T(8,128)(2,1)}, u32[]{:S(2)}) %copy-start.4) | copy-done | bytes 262168
  7.3 0.0 copy-start.5
  7.3 0.7 %copy-done.5 = s32[6,128]{1,0:T(8,128)S(1)} copy-done((s32[6,128]{1,0:T(8,128)S(1)}, s32[6,128]{1,0:T(8,128)}, u32[]{:S(2)}) %copy-start.5) | copy-done | bytes 3096
  8.0 0.0 copy-start.6
  8.0 0.7 %copy-done.6 = f32[1024]{0:T(1024)S(1)} copy-done((f32[1024]{0:T(1024)S(1)}, f32[1024]{0:T(1024)}, u32[]{:S(2)}) %copy-start.6) | copy-done | bytes 4120
  8.7 0.0 copy-start.7
  8.7 0.7 %copy-done.7 = s32[6]{0:T(128)S(1)} copy-done((s32[6]{0:T(128)S(1)}, s32[6]{0:T(128)}, u32[]{:S(2)}) %copy-start.7) | copy-done | bytes 48
  9.3 0.0 copy-start.8
  9.3 0.7 %copy-done.8 = s32[3]{0:T(128)S(1)} copy-done((s32[3]{0:T(128)S(1)}, s32[3]{0:T(128)}, u32[]{:S(2)}) %copy-start.8) | copy-done | bytes 36
  10.0 34.6 %shard_map.121 = (bf16[128,1024]{1,0:T(8,128)(2,1)S(1)}, bf16[1024,1024]{1,0:T(8,128)(2,1)S(1)}, bf16[128,1024]{1,0:T(8,128)(2,1)S(1)}) custom-call(s32[6]{0:T(128)S(1)} %copy-done.7, s32[3]{0:T(128)S(1)} %copy-done.8, s32[6,128]{1,0:T(8,128)S(1)} %copy-done.5, f32[1,1024]{1,0:T(1,128)S(1)} %bitcast.1, bf16[1024,1024]{1,0:T(8,128)(2,1)S(1)} %copy-done, ...), custom_call_target="tpu_custom_call" | custom-call | flops 5368709120 | bytes 12582912 | tf_op jit(solution)/shard_map/pallas_call | solution.py:281
  44.6 0.7 %copy.16 = bf16[128,1024]{1,0:T(8,128)(2,1)} copy(bf16[128,1024]{1,0:T(8,128)(2,1)S(1)} %get-tuple-element.6) | data formatting | bytes 524288
  45.3 1.3 %copy.17 = bf16[1024,1024]{1,0:T(8,128)(2,1)} copy(bf16[1024,1024]{1,0:T(8,128)(2,1)S(1)} %get-tuple-element.7) | data formatting | bytes 4194304
  46.6 0.7 %copy.18 = bf16[128,1024]{1,0:T(8,128)(2,1)} copy(bf16[128,1024]{1,0:T(8,128)(2,1)S(1)} %get-tuple-element.8) | data formatting | bytes 524288
Async XLA Ops:
  0.6 1.6 %copy-start = (bf16[1024,1024]{1,0:T(8,128)(2,1)S(1)}, bf16[1024,1024]{1,0:T(8,128)(2,1)}, u32[]{:S(2)}) copy-start(bf16[1024,1024]{1,0:T(8,128)(2,1)} %x_hbm.1) | copy-start | bytes 6291460
  2.2 1.6 %copy-start.1 = (bf16[1024,1024]{1,0:T(8,128)(2,1)S(1)}, bf16[1024,1024]{1,0:T(8,128)(2,1)}, u32[]{:S(2)}) copy-start(bf16[1024,1024]{1,0:T(8,128)(2,1)} %wsrc_hbm.1) | copy-start | bytes 6291460
  3.8 1.6 %copy-start.2 = (bf16[1024,1024]{1,0:T(8,128)(2,1)S(1)}, bf16[1024,1024]{1,0:T(8,128)(2,1)}, u32[]{:S(2)}) copy-start(bf16[1024,1024]{1,0:T(8,128)(2,1)} %wdst_hbm.1) | copy-start | bytes 6291460
  5.4 0.9 %copy-start.3 = (bf16[128,1024]{1,0:T(8,128)(2,1)S(1)}, bf16[128,1024]{1,0:T(8,128)(2,1)}, u32[]{:S(2)}) copy-start(bf16[128,1024]{1,0:T(8,128)(2,1)} %feats_hbm.1) | copy-start | bytes 786436
  6.4 0.9 %copy-start.4 = (bf16[128,1024]{1,0:T(8,128)(2,1)S(1)}, bf16[128,1024]{1,0:T(8,128)(2,1)}, u32[]{:S(2)}) copy-start(bf16[128,1024]{1,0:T(8,128)(2,1)} %cot_hbm.1) | copy-start | bytes 786436
  7.3 0.7 %copy-start.5 = (s32[6,128]{1,0:T(8,128)S(1)}, s32[6,128]{1,0:T(8,128)}, u32[]{:S(2)}) copy-start(s32[6,128]{1,0:T(8,128)} %rows_ref.1) | copy-start | bytes 9220
  8.0 0.7 %copy-start.6 = (f32[1024]{0:T(1024)S(1)}, f32[1024]{0:T(1024)}, u32[]{:S(2)}) copy-start(f32[1024]{0:T(1024)} %param.16) | copy-start | bytes 12292
  8.7 0.7 %copy-start.7 = (s32[6]{0:T(128)S(1)}, s32[6]{0:T(128)}, u32[]{:S(2)}) copy-start(s32[6]{0:T(128)} %tile_src.1) | copy-start | bytes 76
  9.3 0.7 %copy-start.8 = (s32[3]{0:T(128)S(1)}, s32[3]{0:T(128)}, u32[]{:S(2)}) copy-start(s32[3]{0:T(128)} %tile_count.1) | copy-start | bytes 40

commit v2 on v1

--- a/solution.py
+++ b/solution.py
@@ -9,6 +9,7 @@
 
 NODES = "nodes"
 COLS = 256
+PIECES = 8
 F32 = jnp.float32
 BF16 = jnp.bfloat16
 
@@ -106,7 +107,7 @@
     def send(kind, way, src, landing):
         return pltpu.make_async_remote_copy(
             src_ref=src,
-            dst_ref=landing.at[way],
+            dst_ref=landing.at[pl.ds(way * blk, blk)],
             send_sem=send_sem.at[kind, way],
             recv_sem=recv_sem.at[kind, way],
             device_id={NODES: right if way == 0 else left},
@@ -115,8 +116,8 @@
 
     feat_sends = [send(0, way, feats_hbm, feats_in) for way in range(2)]
     cot_sends = [send(1, way, cot_hbm, cot_in) for way in range(2)]
-    s_sends = [send(2, way, s_send.at[way], s_in) for way in range(2)]
-    p_sends = [send(3, way, p_send.at[way], p_in) for way in range(2)]
+    s_sends = [send(2, way, s_send.at[pl.ds(way * blk, blk)], s_in) for way in range(2)]
+    p_sends = [send(3, way, p_send.at[pl.ds(way * blk, blk)], p_in) for way in range(2)]
     for copy in feat_sends:
         copy.start()
 
@@ -131,8 +132,8 @@
         pick[t * blk : (t + 1) * blk, :blk] = turned
         pick[t * blk : (t + 1) * blk, blk:] = turned
 
-    def chunk(i):
-        return pl.ds(pl.multiple_of(i * COLS, COLS), COLS)
+    def chunks(total):
+        return [slice(i, i + COLS) for i in range(0, total, COLS)]
 
     def share(t, b):
         source = jnp.full((1, COLS), tile_src[t], jnp.int32)
@@ -140,9 +141,7 @@
 
     load_x.wait()
 
-    @pl.loop(0, width // COLS)
-    def _(i):
-        at = chunk(i)
+    for at in chunks(width):
         for t in range(slots):
             tile = share(t, 0).astype(BF16) * x_v[:blk, at]
             for b in range(1, grid_blocks):
@@ -151,67 +150,62 @@
 
     load_wsrc.wait()
 
-    @pl.loop(0, hidden_width // COLS)
-    def _(i):
-        at = chunk(i)
+    for at in chunks(hidden_width):
         pre[:, at] = nn_dot(xt[...], wsrc[:, at]) + bias_ref[:, at]
 
-    def hidden_part(o, feats_ref, s_ref):
-        lines = slice(o * per, (o + 1) * per)
-
-        @pl.loop(0, hidden_width // COLS)
-        def _(i):
-            at = chunk(i)
+    def hidden_part(dests, feats_ref, s_ref):
+        for at in chunks(hidden_width):
             h = nn_dot(feats_ref[...], wdst[:, at])
-            act = pre[lines, at] + nn_dot(pick[lines, :], high_low(h))
-            sig = 0.5 * jnp.tanh(0.5 * act) + 0.5
-            hidden = act * sig
-            pre[lines, at] = sig + hidden * (1.0 - sig)
-            s_ref[:, at] = nn_dot(spread[o], hidden.astype(BF16)).astype(s_ref.dtype)
-
-    def grad_part(o, cot_ref, p_ref):
-        lines = slice(o * per, (o + 1) * per)
-
-        @pl.loop(0, hidden_width // COLS)
-        def _(i):
-            at = chunk(i)
+            for k, o in enumerate(dests):
+                lines = slice(o * per, (o + 1) * per)
+                act = pre[lines, at] + nn_dot(pick[lines, :], high_low(h[k * blk : (k + 1) * blk]))
+                sig = 0.5 * jnp.tanh(0.5 * act) + 0.5
+                hidden = act * sig
+                pre[lines, at] = sig + hidden * (1.0 - sig)
+                back = len(dests) - 1 - k
+                s_ref[back * blk : (back + 1) * blk, at] = nn_dot(
+                    spread[o], hidden.astype(BF16)
+                ).astype(s_ref.dtype)
+
+    def grad_part(dests, cot_ref, p_ref):
+        for at in chunks(hidden_width):
             g = nt_dot(cot_ref[...], wout[at, :])
-            grad = (nn_dot(pick[lines, :], high_low(g)) * pre[lines, at]).astype(BF16)
-            pg[lines, at] = grad
-            p_ref[:, at] = nn_dot(spread[o], grad).astype(p_ref.dtype)
+            for k, o in enumerate(dests):
+                lines = slice(o * per, (o + 1) * per)
+                picked = nn_dot(pick[lines, :], high_low(g[k * blk : (k + 1) * blk]))
+                grad = (picked * pre[lines, at]).astype(BF16)
+                pg[lines, at] = grad
+                back = len(dests) - 1 - k
+                p_ref[back * blk : (back + 1) * blk, at] = nn_dot(spread[o], grad).astype(
+                    p_ref.dtype
+                )
 
     load_feats.wait()
     load_wdst.wait()
-    hidden_part(own, feats, s_own)
-
+    hidden_part((own,), feats, s_own)
     for way in range(2):
         feat_sends[way].wait_send()
         cot_sends[way].start()
-
-    feat_sends[0].wait_recv()
-    hidden_part(own - 1, feats_in.at[0], s_send.at[1])
-    feat_sends[1].wait_recv()
-    hidden_part(own + 1, feats_in.at[1], s_send.at[0])
-
     load_cot.wait()
     load_wout.wait()
-    grad_part(own, cot, p_own)
-
-    for way in range(2):
-        cot_sends[way].wait_send()
+    grad_part((own,), cot, p_own)
+
+
+    for way in range(2):
+        feat_sends[way].wait_recv()
+    hidden_part((own - 1, own + 1), feats_in, s_send)
+
+    for way in range(2):
         s_sends[way].start()
 
-    cot_sends[0].wait_recv()
-    grad_part(own - 1, cot_in.at[0], p_send.at[1])
-    cot_sends[1].wait_recv()
-    grad_part(own + 1, cot_in.at[1], p_send.at[0])
+    for way in range(2):
+        cot_sends[way].wait_recv()
+    grad_part((own - 1, own + 1), cot_in, p_send)
 
     for way in range(2):
         p_sends[way].start()
 
-    @pl.loop(0, width // COLS)
-    def _(i):
-        at = chunk(i)
+    for at in chunks(width):
         gt[...] = nt_dot(pg[...], wsrc[at, :])
         for b in range(grid_blocks):
             total = share(0, b) * gt[:blk, :]
@@ -224,12 +218,10 @@
 
     for way in range(2):
         s_sends[way].wait_recv()
-    s_all = high_low(s_own[...] + s_in[0].astype(F32) + s_in[1].astype(F32))
+    s_all = high_low(s_own[...] + s_in[:blk].astype(F32) + s_in[blk:].astype(F32))
     xt[: 2 * blk, :] = s_all
 
-    @pl.loop(0, width // COLS)
-    def _(i):
-        at = chunk(i)
+    for at in chunks(width):
         both = nn_dot(xt[: 2 * blk, :], wout[:, at])
         mo[:, at] = (feats[:, at].astype(F32) + both[:blk] + both[blk:]).astype(BF16)
 
@@ -238,16 +230,15 @@
 
     for way in range(2):
         p_sends[way].wait_recv()
-    xt[:blk, :] = (p_own[...] + p_in[0].astype(F32) + p_in[1].astype(F32)).astype(BF16)
-
-    @pl.loop(0, width // COLS)
-    def _(i):
-        at = chunk(i)
+    xt[:blk, :] = (p_own[...] + p_in[:blk].astype(F32) + p_in[blk:].astype(F32)).astype(BF16)
+
+    for at in chunks(width):
         mg[:, at] = (cot[:, at].astype(F32) + nt_dot(xt[:blk, :], wdst[at, :])).astype(BF16)
 
     store_cot = pltpu.make_async_copy(mg, mesh_grad, store_sem.at[2])
     store_cot.start()
     for way in range(2):
+        cot_sends[way].wait_send()
         s_sends[way].wait_send()
         p_sends[way].wait_send()
     store_grid.wait()
@@ -278,7 +269,7 @@
     scalar = pl.BlockSpec(memory_space=pltpu.SMEM)
     vector = pl.BlockSpec(memory_space=pltpu.VMEM)
     flops = 2 * width * hid * (2 * slots * blk + 8 * blk)
-    return pl.pallas_call(
+    outs = pl.pallas_call(
         functools.partial(kernel, n),
         out_shape=(
             jax.ShapeDtypeStruct(mesh_feats.shape, BF16),
@@ -301,12 +292,12 @@
             pltpu.VMEM((slots * blk, 2 * blk), BF16),
             pltpu.VMEM((blk, hid), F32),
             pltpu.VMEM((blk, hid), F32),
-            pltpu.VMEM((2, blk, hid), BF16),
-            pltpu.VMEM((2, blk, hid), BF16),
-            pltpu.VMEM((2, blk, width), BF16),
-            pltpu.VMEM((2, blk, width), BF16),
-            pltpu.VMEM((2, blk, hid), BF16),
-            pltpu.VMEM((2, blk, hid), BF16),
+            pltpu.VMEM((2 * blk, hid), BF16),
+            pltpu.VMEM((2 * blk, hid), BF16),
+            pltpu.VMEM((2 * blk, width), BF16),
+            pltpu.VMEM((2 * blk, width), BF16),
+            pltpu.VMEM((2 * blk, hid), BF16),
+            pltpu.VMEM((2 * blk, hid), BF16),
             pltpu.VMEM((slots * blk, COLS), F32),
             pltpu.VMEM(grid_feats.shape, BF16),
             pltpu.VMEM((blk, width), BF16),
@@ -317,7 +308,7 @@
             pltpu.SemaphoreType.DMA((4, 2)),
         ],
         compiler_params=pltpu.CompilerParams(
-            collective_id=0, has_side_effects=True, vmem_limit_bytes=44 * 1024 * 1024
+            collective_id=0, has_side_effects=True, vmem_limit_bytes=63 * 1024 * 1024
         ),
         cost_estimate=pl.CostEstimate(
             flops=flops, bytes_accessed=12 * 1024 * 1024, transcendentals=slots * blk * hid
@@ -334,6 +325,38 @@
         w_dst,
         w_out,
     )
+    return pl.pallas_call(
+        copy_out,
+        out_shape=tuple(jax.ShapeDtypeStruct(o.shape, o.dtype) for o in outs),
+        in_specs=[anywhere] * 3,
+        out_specs=(anywhere,) * 3,
+        scratch_shapes=[pltpu.VMEM(o.shape, o.dtype) for o in outs]
+        + [pltpu.SemaphoreType.DMA((3, PIECES))] * 2,
+        compiler_params=pltpu.CompilerParams(vmem_limit_bytes=63 * 1024 * 1024),
+        cost_estimate=pl.CostEstimate(flops=0, bytes_accessed=5 * 1024 * 1024, transcendentals=0),
+    )(*outs)
+
+
+def copy_out(*refs):
+    held, in_sem, out_sem = refs[6:9], refs[9], refs[10]
+    parts = []
+    for k in range(3):
+        rows = refs[k].shape[0] // PIECES
+        for j in range(PIECES):
+            part = pl.ds(j * rows, rows)
+            parts.append(
+                (
+                    pltpu.make_async_copy(refs[k].at[part], held[k].at[part], in_sem.at[k, j]),
+                    pltpu.make_async_copy(held[k].at[part], refs[3 + k].at[part], out_sem.at[k, j]),
+                )
+            )
+    for arrive, _ in parts:
+        arrive.start()
+    for arrive, leave in parts:
+        arrive.wait()
+        leave.start()
+    for _, leave in parts:
+        leave.wait()
 
 
 def solution(mesh):

time: 47.7 us -> 34.9 us (0.73)
  local copies, waits for them, and re-layouts: 12.1 us -> 0 us
  Pallas kernels: 34.6 us -> 34 us
    unnamed x21 -> x0, local copies, waits for them, and re-layouts: 12.1 us -> none
    pallas_call x1, Pallas kernels: 34.6 us -> 31.1 us  [local(): pl.pallas_call(functools.partial(kernel, n), out_shape=(jax.ShapeDtypeStr...]
    pallas_call x0 -> x1, Pallas kernels: none -> 2.91 us  [local(): pl.pallas_call(copy_out, out_shape=tuple((jax.ShapeDtypeStruct(o.shape, o...]
where the time goes in v2:
time: 34.9 us; the launch traced here: 34.7 us
  Pallas kernels  34 us (97%)
  between operations  0.64 us (2%)
    pallas_call x1, Pallas kernels, local(): pl.pallas_call(functools.partial(kernel, n), out_shape=(jax.ShapeDtypeStr...  31.1 us
    pallas_call x1, Pallas kernels, local(): pl.pallas_call(copy_out, out_shape=tuple((jax.ShapeDtypeStruct(o.shape, o...  2.91 us

profile of v2, /device:TPU:1, one launch (start us, length us, event | category | flops | bytes accessed | tf_op | source)
XLA Modules:
  0.0 34.7 jit_solution(16184124674146978860)
XLA Ops:
  0.6 31.1 %shard_map.121 = (bf16[128,1024]{1,0:T(8,128)(2,1)}, bf16[1024,1024]{1,0:T(8,128)(2,1)}, bf16[128,1024]{1,0:T(8,128)(2,1)}) custom-call(s32[6]{0:T(128)} %tile_src.1, s32[3]{0:T(128)} %tile_count.1, s32[6,128]{1,0:T(8,128)} %rows_ref.1, f32[1,1024]{1,0:T(1,128)} %bitcast.1, bf16[1024,1024]{1,0:T(8,128)(2,1)} %x_hbm.1, bf16[128,1024]{1,0:T(8,128)(2,1)} %feats_hbm.1, ...), custom_call_target="tpu_custom_call" | custom-call | flops 5368709120 | bytes 12582912 | tf_op jit(solution)/shard_map/pallas_call | solution.py:272
  31.7 2.9 %shard_map.122 = (bf16[128,1024]{1,0:T(8,128)(2,1)}, bf16[1024,1024]{1,0:T(8,128)(2,1)}, bf16[128,1024]{1,0:T(8,128)(2,1)}) custom-call(bf16[128,1024]{1,0:T(8,128)(2,1)} %get-tuple-element.6.refs_0_, bf16[1024,1024]{1,0:T(8,128)(2,1)} %get-tuple-element.7.refs_1_, bf16[128,1024]{1,0:T(8,128)(2,1)} %get-tuple-element.8.refs_2_), custom_call_target="tpu_custom_call" | custom-call | bytes 5242880 | tf_op jit(solution)/shard_map/pallas_call | solution.py:328
